TPU v7x, 32 devices: a whole 2x2x4 slice. The times are simulated.
32 devices in a mesh: row: 4 (over y, x), col: 8 (over z, core).
Axes of the slice: x: 2, y: 2, z: 4, core: 2. Of those that a mesh axis runs over, the one named last changes fastest.
Arguments:
- tokens: bfloat16 [128, 256, 1024], P(('row', 'col')), may hold values from -7 to 7
- phi: bfloat16 [1024, 32], replicated, may hold values from -5 to 5
- w_in: bfloat16 [32, 1024, 2048], P(('row', 'col')), may hold values from -0.1875 to 0.1875
- w_out: bfloat16 [32, 2048, 1024], P(('row', 'col')), may hold values from -0.125 to 0.125
- cotangent: bfloat16 [128, 256, 1024], P(('row', 'col')), may hold values from -6 to 6
Outputs:
- mixed: bfloat16 [128, 256, 1024], P(('row', 'col'))
- grad_tokens: bfloat16 [128, 256, 1024], P(('row', 'col'))
- grad_phi: float32 [1024, 32], P(None, ('row', 'col'))
- grad_w_in: bfloat16 [32, 1024, 2048], P(('row', 'col'))
- grad_w_out: bfloat16 [32, 2048, 1024], P(('row', 'col'))
All inputs are finite; a program needn't handle non-finite values.
Results may differ from a plain program's by a relative error of at most 0.015.
Values may be sent and summed in bfloat16 or wider, within the bound.
A program may use at most 128 MiB of HBM per device.

v0:
```python
import math
import jax
import jax.numpy as jnp
from jax import lax
from jax.sharding import PartitionSpec as P


def gelu_parts(pre_act):
    const = math.sqrt(2.0 / math.pi)
    inner = const * (pre_act + 0.044715 * pre_act**3)
    tanh_val = jnp.tanh(inner)
    value = 0.5 * pre_act * (1.0 + tanh_val)
    slope = 0.5 * (1.0 + tanh_val) + 0.5 * pre_act * (1.0 - tanh_val * tanh_val) * const * (
        1.0 + 3.0 * 0.044715 * pre_act * pre_act
    )
    return (value, slope)


def send_slots(slots):
    return lax.all_to_all(slots, ("row", "col"), split_axis=1, concat_axis=1, tiled=True)


def return_results(slots):
    return lax.all_to_all(slots, ("row", "col"), split_axis=1, concat_axis=1, tiled=True)


def send_out_grads(slots):
    return lax.all_to_all(slots, ("row", "col"), split_axis=1, concat_axis=1, tiled=True)


def return_in_grads(slots):
    return lax.all_to_all(slots, ("row", "col"), split_axis=1, concat_axis=1, tiled=True)


def on_device(tokens, phi, w_in, w_out, cotangent):
    f32 = jnp.float32
    images, patches, feature_dim = tokens.shape
    logits = jnp.einsum("imd,ds->ims", tokens, phi, preferred_element_type=f32)
    dispatch = jax.nn.softmax(logits, axis=1)
    combine = jax.nn.softmax(logits, axis=2)
    dispatch_b = dispatch.astype(jnp.bfloat16)
    combine_b = combine.astype(jnp.bfloat16)
    slot_in = jnp.einsum("ims,imd->isd", dispatch_b, tokens, preferred_element_type=f32).astype(
        jnp.bfloat16
    )
    expert_in = send_slots(slot_in)
    expert_rows = expert_in.reshape(-1, feature_dim)
    weight_a = w_in[0]
    weight_b = w_out[0]
    pre_act = jnp.dot(expert_rows, weight_a, preferred_element_type=f32)
    value, slope = gelu_parts(pre_act)
    hidden = value.astype(jnp.bfloat16)
    expert_out = jnp.dot(hidden, weight_b, preferred_element_type=f32).astype(jnp.bfloat16)
    slot_out = return_results(expert_out.reshape(expert_in.shape))
    mixed = jnp.einsum("ims,isd->imd", combine_b, slot_out, preferred_element_type=f32).astype(
        jnp.bfloat16
    )
    d_slot_out = jnp.einsum(
        "ims,imd->isd", combine_b, cotangent, preferred_element_type=f32
    ).astype(jnp.bfloat16)
    grad_rows = send_out_grads(d_slot_out).reshape(-1, feature_dim)
    d_combine = jnp.einsum("imd,isd->ims", cotangent, slot_out, preferred_element_type=f32)
    d_logits_c = combine * (d_combine - jnp.sum(combine * d_combine, axis=2, keepdims=True))
    grad_b = jnp.einsum("rh,rd->hd", hidden, grad_rows, preferred_element_type=f32).astype(
        jnp.bfloat16
    )
    d_hidden = jnp.einsum("rd,hd->rh", grad_rows, weight_b, preferred_element_type=f32)
    d_pre = (d_hidden * slope).astype(jnp.bfloat16)
    grad_a = jnp.einsum("rd,rh->dh", expert_rows, d_pre, preferred_element_type=f32).astype(
        jnp.bfloat16
    )
    d_rows = jnp.einsum("rh,dh->rd", d_pre, weight_a, preferred_element_type=f32).astype(
        jnp.bfloat16
    )
    d_slot_in = return_in_grads(d_rows.reshape(expert_in.shape))
    d_dispatch = jnp.einsum("imd,isd->ims", tokens, d_slot_in, preferred_element_type=f32)
    d_logits = (
        d_logits_c + dispatch * (d_dispatch - jnp.sum(dispatch * d_dispatch, axis=1, keepdims=True))
    ).astype(jnp.bfloat16)
    grad_tokens = (
        jnp.einsum("ims,isd->imd", dispatch_b, d_slot_in, preferred_element_type=f32)
        + jnp.einsum("ims,ds->imd", d_logits, phi, preferred_element_type=f32)
    ).astype(jnp.bfloat16)
    phi_terms = jnp.einsum("imd,ims->ds", tokens, d_logits, preferred_element_type=f32)
    grad_phi = lax.psum_scatter(phi_terms, ("row", "col"), scatter_dimension=1, tiled=True)
    return (mixed, grad_tokens, grad_phi, grad_a[None], grad_b[None])


def solution(mesh):
    placed = (
        P(("row", "col"), None, None),
        P(),
        P(("row", "col"), None, None),
        P(("row", "col"), None, None),
        P(("row", "col"), None, None),
    )
    return jax.shard_map(
        on_device,
        mesh=mesh,
        in_specs=placed,
        out_specs=(
            P(("row", "col"), None, None),
            P(("row", "col"), None, None),
            P(None, ("row", "col")),
            P(("row", "col"), None, None),
            P(("row", "col"), None, None),
        ),
        check_vma=False,
    )
```

profile of v0, /device:TPU:0, one launch (start us, length us, event | category | flops | bytes accessed | tf_op | source)
XLA Modules:
  0.0 219.8 jit_solution(336582949832847394)
XLA Ops:
  7.2 0.0 copy-start
  7.2 1.6 copy-done
  8.8 1.6 fusion.52
  10.3 0.8 fusion.60
  11.1 0.5 convolution_convert_fusion.2
  11.6 0.9 copy.18
  12.5 7.3 %all-to-all-start = ((bf16[4,32,1024]{2,0,1:T(4,128)(2,1)}), bf16[4,32,1024]{2,0,1:T(4,128)(2,1)S(1)}, u32[]{:S(2)}, u32[]{:S(2)}) async-start(bf16[4,32,1024]{2,0,1:T(4,128)(2,1)} %copy.18), calls=%async_computation | async-start | bytes 524288 | tf_op jit(solution)/shard_map/all_to_all | solution.py:20
  19.8 0.7 fusion.61
  20.5 2.0 convolution_convert_fusion.1
  22.6 0.9 copy.22
  23.5 6.7 %all-to-all-done = bf16[4,32,1024]{2,0,1:T(4,128)(2,1)S(1)} async-done(((bf16[4,32,1024]{2,0,1:T(4,128)(2,1)}), bf16[4,32,1024]{2,0,1:T(4,128)(2,1)S(1)}, u32[]{:S(2)}, u32[]{:S(2)}) %all-to-all-start) | async-done | bytes 262176 | tf_op jit(solution)/shard_map/all_to_all | solution.py:20
  30.2 3.3 %all-to-all-start.2 = ((bf16[4,32,1024]{2,0,1:T(4,128)(2,1)}), bf16[4,32,1024]{2,0,1:T(4,128)(2,1)}, u32[]{:S(2)}, u32[]{:S(2)}) async-start(bf16[4,32,1024]{2,0,1:T(4,128)(2,1)} %copy.22), calls=%async_computation.2 | async-start | bytes 524288 | tf_op jit(solution)/shard_map/all_to_all | solution.py:28
  33.5 0.0 copy-start.7
  33.5 0.1 copy.19
  33.6 3.1 %fusion.10 = f32[128,2048]{1,0:T(8,128)S(1)} fusion(bf16[128,1024]{1,0:T(8,128)(2,1)S(1)} %bitcast.57, bf16[1,1024,2048]{2,1,0:T(8,128)(2,1)} %param.7), kind=kOutput, calls=%fused_computation.10 | convolution fusion | flops 536870912 | bytes 5505024 | tf_op jit(solution)/shard_map/dot_general | solution.py:50
  36.7 0.3 copy-done.7
  37.0 1.6 fusion.21
  38.6 5.3 %all-to-all-done.2 = bf16[4,32,1024]{2,0,1:T(4,128)(2,1)} async-done(((bf16[4,32,1024]{2,0,1:T(4,128)(2,1)}), bf16[4,32,1024]{2,0,1:T(4,128)(2,1)}, u32[]{:S(2)}, u32[]{:S(2)}) %all-to-all-start.2) | async-done | bytes 262176 | tf_op jit(solution)/shard_map/all_to_all | solution.py:28
  43.9 1.0 copy.23
  44.9 0.0 copy-start.2
  44.9 0.0 copy-start.6
  44.9 4.9 %fusion.15 = bf16[128,2048]{1,0:T(8,128)(2,1)} fusion(bf16[128,1024]{1,0:T(8,128)(2,1)S(1)} %bitcast.59, bf16[1,2048,1024]{2,1,0:T(8,128)(2,1)} %param.8, f32[128,2048]{1,0:T(8,128)S(1)} %fusion.10), kind=kOutput, calls=%fused_computation.16 | convolution fusion | flops 541851648 | bytes 6029312 | tf_op jit(solution)/shard_map/rd,hd->rh/dot_general | solution.py:67
  49.8 0.0 copy-done.2
  49.8 0.0 copy-done.6
  49.8 0.9 copy.20
  50.8 3.3 %all-to-all-start.1 = ((bf16[4,32,1024]{2,0,1:T(4,128)(2,1)}), bf16[4,32,1024]{2,0,1:T(4,128)(2,1)}, u32[]{:S(2)}, u32[]{:S(2)}) async-start(bf16[4,32,1024]{2,0,1:T(4,128)(2,1)} %copy.20), calls=%async_computation.1 | async-start | bytes 524288 | tf_op jit(solution)/shard_map/all_to_all | solution.py:24
  54.1 0.0 copy-start.1
  54.1 0.0 copy-start.3
  54.1 3.9 %fusion.18 = bf16[128,1024]{1,0:T(8,128)(2,1)S(1)} fusion(bf16[128,2048]{1,0:T(8,128)(2,1)} %fusion.15, bf16[1,1024,2048]{2,1,0:T(8,128)(2,1)} %param.7), kind=kOutput, calls=%fused_computation.22 | convolution fusion | flops 537001984 | bytes 4980736 | tf_op jit(solution)/shard_map/rh,dh->rd/dot_general | solution.py:72
  58.0 0.9 copy.24
  58.9 3.3 %convert_bitcast_fusion.1 = bf16[1,1024,2048]{2,1,0:T(8,128)(2,1)} fusion(bf16[128,1024]{1,0:T(8,128)(2,1)S(1)} %bitcast.58, bf16[128,2048]{1,0:T(8,128)(2,1)S(1)} %copy-done.1), kind=kOutput, calls=%fused_computation.13 | convolution fusion | flops 538968064 | bytes 4980736 | tf_op jit(solution)/shard_map/rd,rh->dh/dot_general | solution.py:69
  62.2 3.3 %convert_bitcast_fusion = bf16[1,2048,1024]{2,1,0:T(8,128)(2,1)} fusion(bf16[128,1024]{1,0:T(8,128)(2,1)S(1)} %bitcast.60, f32[128,2048]{1,0:T(8,128)S(1)} %fusion.10), kind=kOutput, calls=%fused_computation.12 | convolution fusion | flops 541327360 | bytes 5505024 | tf_op jit(solution)/shard_map/rh,rd->hd/dot_general | solution.py:64
  65.6 0.0 all-to-all-done.1
  65.6 5.8 %all-to-all-start.3 = ((bf16[4,32,1024]{2,0,1:T(4,128)(2,1)}), bf16[4,32,1024]{2,0,1:T(4,128)(2,1)S(1)}, u32[]{:S(2)}, u32[]{:S(2)}) async-start(bf16[4,32,1024]{2,0,1:T(4,128)(2,1)} %copy.24), calls=%async_computation.3 | async-start | bytes 524288 | tf_op jit(solution)/shard_map/all_to_all | solution.py:32
  71.3 0.2 all-reduce.3.cloned.1.call-start
  71.6 2.4 %convolution_bitcast_fusion.1 = f32[4,256,32]{1,2,0:T(8,128)S(1)} fusion(bf16[4,256,1024]{2,1,0:T(8,128)(2,1)} %param.9, bf16[4,32,1024]{2,0,1:T(4,128)(2,1)} %all-to-all-done.1), kind=kOutput, calls=%fused_computation.27 | convolution fusion | flops 67108864 | bytes 2490368 | tf_op jit(solution)/shard_map/imd,isd->ims/dot_general | solution.py:62
  74.0 1.0 fusion.32
  75.0 0.0 copy-start.5
  75.0 6.7 %all-to-all-done.3 = bf16[4,32,1024]{2,0,1:T(4,128)(2,1)S(1)} async-done(((bf16[4,32,1024]{2,0,1:T(4,128)(2,1)}), bf16[4,32,1024]{2,0,1:T(4,128)(2,1)S(1)}, u32[]{:S(2)}, u32[]{:S(2)}) %all-to-all-start.3) | async-done | bytes 262176 | tf_op jit(solution)/shard_map/all_to_all | solution.py:32
  81.7 0.7 convolution_bitcast_fusion
  82.4 0.0 copy-done.4
  82.5 1.2 convolution_bitcast_fusion.2
  83.7 2.8 %fusion.46 = f32[4,256,1024]{2,1,0:T(8,128)} fusion(bf16[4,32,1024]{2,0,1:T(4,128)(2,1)S(1)} %all-to-all-done.3, f32[4,32]{1,0:T(4,128)S(1)} %get-tuple-element.5, f32[4,256,32]{1,2,0:T(8,128)S(1)} %fusion.52), kind=kOutput, calls=%fused_computation.49 | convolution fusion | flops 67207552 | bytes 4588032 | tf_op jit(solution)/shard_map/ims,isd->imd/dot_general | solution.py:81
  86.5 4.5 %add_convert_fusion = bf16[4,256,1024]{2,1,0:T(8,128)(2,1)} fusion(f32[4,256,1024]{2,1,0:T(8,128)} %fusion.46, f32[4,256,32]{1,2,0:T(8,128)S(1)} %fusion.32, f32[4,256,32]{1,2,0:T(8,128)S(1)} %convolution_bitcast_fusion, bf16[1024,32]{0,1:T(8,128)(2,1)S(1)} %copy-done.5, f32[4,256,32]{1,2,0:T(8,128)S(1)} %copy-done.4, f32[4,32]{1,0:T(4,128)S(1)} %get-tuple-element.5), kind=kOutput, calls=%fused_computation.14 | convolution fusion | flops 69435776 | bytes 6750720 | tf_op jit(solution)/shard_map/ims,ds->imd/dot_general | solution.py:82
  91.0 0.0 all-reduce.3.cloned.1.call-update
  91.0 3.0 %convolution_convert_fusion = bf16[4,256,1024]{2,1,0:T(8,128)(2,1)} fusion(bf16[4,32,1024]{2,0,1:T(4,128)(2,1)} %all-to-all-done.1, f32[4,256]{1,0:T(4,128)S(1)} %get-tuple-element.7, f32[4,256,32]{1,2,0:T(8,128)S(1)} %fusion.52), kind=kOutput, calls=%fused_computation.17 | convolution fusion | flops 68256800 | bytes 2494464 | tf_op jit(solution)/shard_map/ims,isd->imd/dot_general | solution.py:55
  94.1 117.5 %all-reduce.3.cloned.1.call-done = f32[1024,32]{0,1:T(8,128)} async-done(((f32[1024,32]{0,1:T(8,128)}), f32[1024,32]{0,1:T(8,128)}) %all-reduce.3.cloned.1.call-update) | async-done | bytes 131088
  211.6 1.4 constant_dynamic-slice_fusion
  (4 shorter events, 0.0 us)
Async XLA Ops:
  7.2 1.6 copy-start
  12.5 17.7 %all-to-all-start = ((bf16[4,32,1024]{2,0,1:T(4,128)(2,1)}), bf16[4,32,1024]{2,0,1:T(4,128)(2,1)S(1)}, u32[]{:S(2)}, u32[]{:S(2)}) async-start(bf16[4,32,1024]{2,0,1:T(4,128)(2,1)} %copy.18), calls=%async_computation | async-start | bytes 524288 | tf_op jit(solution)/shard_map/all_to_all | solution.py:20
  30.2 13.7 %all-to-all-start.2 = ((bf16[4,32,1024]{2,0,1:T(4,128)(2,1)}), bf16[4,32,1024]{2,0,1:T(4,128)(2,1)}, u32[]{:S(2)}, u32[]{:S(2)}) async-start(bf16[4,32,1024]{2,0,1:T(4,128)(2,1)} %copy.22), calls=%async_computation.2 | async-start | bytes 524288 | tf_op jit(solution)/shard_map/all_to_all | solution.py:28
  33.5 3.5 %copy-start.7 = (bf16[1,2048,1024]{2,1,0:T(8,128)(2,1)S(1)}, bf16[1,2048,1024]{2,1,0:T(8,128)(2,1)}, u32[]{:S(2)}) copy-start(bf16[1,2048,1024]{2,1,0:T(8,128)(2,1)} %param.8) | copy-start | bytes 12582916
  44.9 4.9 %copy-start.2 = (bf16[4,32,1024]{2,1,0:T(8,128)(2,1)}, bf16[4,32,1024]{2,1,0:T(8,128)(2,1)S(1)}, u32[]{:S(2)}) copy-start(bf16[4,32,1024]{2,1,0:T(8,128)(2,1)S(1)} %copy.23) | copy-start | bytes 786436
  44.9 4.9 %copy-start.6 = (bf16[128,1024]{1,0:T(8,128)(2,1)S(1)}, bf16[128,1024]{1,0:T(8,128)(2,1)}, u32[]{:S(2)}) copy-start(bf16[128,1024]{1,0:T(8,128)(2,1)} %fusion.21) | copy-start | bytes 786436
  50.8 14.8 %all-to-all-start.1 = ((bf16[4,32,1024]{2,0,1:T(4,128)(2,1)}), bf16[4,32,1024]{2,0,1:T(4,128)(2,1)}, u32[]{:S(2)}, u32[]{:S(2)}) async-start(bf16[4,32,1024]{2,0,1:T(4,128)(2,1)} %copy.20), calls=%async_computation.1 | async-start | bytes 524288 | tf_op jit(solution)/shard_map/all_to_all | solution.py:24
  54.1 4.9 %copy-start.1 = (bf16[128,2048]{1,0:T(8,128)(2,1)S(1)}, bf16[128,2048]{1,0:T(8,128)(2,1)}, u32[]{:S(2)}) copy-start(bf16[128,2048]{1,0:T(8,128)(2,1)} %fusion.15) | copy-start | bytes 1572868
  54.1 8.1 %copy-start.3 = (bf16[4,32,1024]{2,1,0:T(8,128)(2,1)S(1)}, bf16[4,32,1024]{2,1,0:T(8,128)(2,1)}, u32[]{:S(2)}) copy-start(bf16[4,32,1024]{2,1,0:T(8,128)(2,1)} %copy-done.2) | copy-start | bytes 786436
  65.6 16.9 %copy-start.4 = (f32[4,256,32]{1,2,0:T(8,128)S(1)}, f32[4,256,32]{1,2,0:T(8,128)}, u32[]{:S(2)}) copy-start(f32[4,256,32]{1,2,0:T(8,128)} %get-tuple-element.6) | copy-start | bytes 393220
  65.6 16.2 %all-to-all-start.3 = ((bf16[4,32,1024]{2,0,1:T(4,128)(2,1)}), bf16[4,32,1024]{2,0,1:T(4,128)(2,1)S(1)}, u32[]{:S(2)}, u32[]{:S(2)}) async-start(bf16[4,32,1024]{2,0,1:T(4,128)(2,1)} %copy.24), calls=%async_computation.3 | async-start | bytes 524288 | tf_op jit(solution)/shard_map/all_to_all | solution.py:32
  71.3 140.2 %all-reduce.3.cloned.1.call-start = ((), (), s32[]{:S(2)}) async-start(), calls=%async_computation.4 | async-start | bytes 262144
  75.0 11.5 %copy-start.5 = (bf16[1024,32]{0,1:T(8,128)(2,1)S(1)}, bf16[1024,32]{0,1:T(8,128)(2,1)}, u32[]{:S(2)}) copy-start(bf16[1024,32]{0,1:T(8,128)(2,1)} %param.6) | copy-start | bytes 196612
Sparse Core Ops, SparseCore 0:
  91.2 120.3 all-reduce.2
where the time goes:
time: 220 us
  waiting for transfers between devices  136 us (62%)
  matrix products  38.9 us (18%)
  starting transfers between devices  19.9 us (9%)
  between operations  14.2 us (6%)
  local copies, waits for them, and re-layouts  8.05 us (4%)
  other arithmetic  2.51 us (1%)
    unnamed x2, waiting for transfers between devices  118 us
    all_to_all x1, starting transfers between devices, send_slots(): lax.all_to_all(slots, ('row', 'col'), split_axis=1, concat_axis=1, tiled=...  7.3 us
    all_to_all x1, waiting for transfers between devices, send_slots(): lax.all_to_all(slots, ('row', 'col'), split_axis=1, concat_axis=1, tiled=...  6.71 us
    all_to_all x1, waiting for transfers between devices, return_in_grads(): lax.all_to_all(slots, ('row', 'col'), split_axis=1, concat_axis=1, tiled=...  6.69 us
    all_to_all x1, starting transfers between devices, return_in_grads(): lax.all_to_all(slots, ('row', 'col'), split_axis=1, concat_axis=1, tiled=...  5.76 us
    all_to_all x1, waiting for transfers between devices, send_out_grads(): lax.all_to_all(slots, ('row', 'col'), split_axis=1, concat_axis=1, tiled=...  5.3 us
    dot_general x1, matrix products, on_device(): jnp.einsum('rd,hd->rh', grad_rows, weight_b, preferred_element_type=f32)  4.91 us
    dot_general x1, matrix products, on_device(): jnp.einsum('ims,ds->imd', d_logits, phi, preferred_element_type=f32)  4.47 us
  transfers between devices with their start and end apart: 5, of which 4 were waited for; matrix products, arithmetic and copies ran while one was open for 12% of the time, Pallas kernels for 0%

commit v1 on v0

--- a/solution.py
+++ b/solution.py
@@ -17,7 +17,12 @@
 
 
 def send_slots(slots):
-    return lax.all_to_all(slots, ("row", "col"), split_axis=1, concat_axis=1, tiled=True)
+    return jnp.concatenate(
+        lax.all_to_all(
+            jnp.stack(jnp.split(slots, lax.axis_size(("row", "col")), axis=1)), ("row", "col"), 0, 0
+        ),
+        axis=1,
+    )
 
 
 def return_results(slots):

time: 220 us -> 232 us (1.055)
  local copies, waits for them, and re-layouts: 8.05 us -> 27 us
  waiting for transfers between devices: 136 us -> 129 us
    unnamed x17 -> x48, local copies, waits for them, and re-layouts: 3.28 us -> 22 us
    unnamed x2, waiting for transfers between devices: 118 us -> 110 us
  transfers between devices with their start and end apart: 5 -> 5, of which waited for: 4 -> 4; matrix products, arithmetic and copies ran while one was open for 12% -> 15% of each run, Pallas kernels for 0% -> 0%
where the time goes in v1:
time: 232 us; the launch traced here: 231 us
  waiting for transfers between devices  129 us (56%)
  matrix products  39 us (17%)
  local copies, waits for them, and re-layouts  27 us (12%)
  starting transfers between devices  19.9 us (9%)
  between operations  14.2 us (6%)
  other arithmetic  2.51 us (1%)
    unnamed x2, waiting for transfers between devices  110 us
    unnamed x48, local copies, waits for them, and re-layouts  22 us
    all_to_all x1, starting transfers between devices, send_slots(): lax.all_to_all(jnp.stack(jnp.split(slots, lax.axis_size(('row', 'col')),...  7.3 us
    all_to_all x1, waiting for transfers between devices, send_slots(): lax.all_to_all(jnp.stack(jnp.split(slots, lax.axis_size(('row', 'col')),...  6.71 us
    all_to_all x1, waiting for transfers between devices, return_in_grads(): lax.all_to_all(slots, ('row', 'col'), split_axis=1, concat_axis=1, tiled=...  6.69 us
    all_to_all x1, starting transfers between devices, return_in_grads(): lax.all_to_all(slots, ('row', 'col'), split_axis=1, concat_axis=1, tiled=...  5.76 us
    all_to_all x1, waiting for transfers between devices, send_out_grads(): lax.all_to_all(slots, ('row', 'col'), split_axis=1, concat_axis=1, tiled=...  5.3 us
    dot_general x1, matrix products, on_device(): jnp.einsum('rd,hd->rh', grad_rows, weight_b, preferred_element_type=f32)  4.91 us
  transfers between devices with their start and end apart: 5, of which 4 were waited for; matrix products, arithmetic and copies ran while one was open for 15% of the time, Pallas kernels for 0%

profile of v1, /device:TPU:0, one launch (start us, length us, event | category | flops | bytes accessed | tf_op | source)
XLA Modules:
  0.0 231.4 jit_solution(11266313475788168160)
XLA Ops:
  7.2 1.6 copy-done
  8.8 1.6 fusion.52
  10.3 0.8 fusion.62
  12.2 0.6 constant_dynamic-update-slice_fusion.31
  14.0 0.6 constant_dynamic-update-slice_fusion.28
  14.6 0.6 constant_dynamic-update-slice_fusion.27
  15.2 0.6 constant_dynamic-update-slice_fusion.26
  15.8 0.6 constant_dynamic-update-slice_fusion.25
  16.4 0.6 constant_dynamic-update-slice_fusion.24
  17.0 0.6 constant_dynamic-update-slice_fusion.23
  20.0 0.6 constant_dynamic-update-slice_fusion.18
  20.6 0.6 constant_dynamic-update-slice_fusion.17
  21.2 0.6 constant_dynamic-update-slice_fusion.16
  21.8 0.6 constant_dynamic-update-slice_fusion.15
  22.4 0.6 constant_dynamic-update-slice_fusion.14
  25.4 0.6 constant_dynamic-update-slice_fusion.9
  26.0 0.6 constant_dynamic-update-slice_fusion.8
  26.6 0.6 constant_dynamic-update-slice_fusion.7
  27.2 0.6 constant_dynamic-update-slice_fusion.6
  27.8 0.6 constant_dynamic-update-slice_fusion.5
  31.5 7.3 %all-to-all-start = ((bf16[32,4,1,1024]{3,1,2,0:T(4,128)(2,1)}), bf16[32,4,1,1024]{3,1,2,0:T(4,128)(2,1)S(1)}, u32[]{:S(2)}, u32[]{:S(2)}) async-start(bf16[32,4,1,1024]{3,1,2,0:T(4,128)(2,1)} %constant_dynamic-update-slice_fusion), calls=%async_computation | async-start | bytes 524288 | tf_op jit(solution)/shard_map/all_to_all | solution.py:21
  38.8 0.7 fusion.63
  39.5 2.0 convolution_convert_fusion.1
  41.5 0.9 copy.540
  42.4 6.7 %all-to-all-done = bf16[32,4,1,1024]{3,1,2,0:T(4,128)(2,1)S(1)} async-done(((bf16[32,4,1,1024]{3,1,2,0:T(4,128)(2,1)}), bf16[32,4,1,1024]{3,1,2,0:T(4,128)(2,1)S(1)}, u32[]{:S(2)}, u32[]{:S(2)}) %all-to-all-start) | async-done | bytes 262176 | tf_op jit(solution)/shard_map/all_to_all | solution.py:21
  49.2 3.3 %all-to-all-start.2 = ((bf16[4,32,1024]{2,0,1:T(4,128)(2,1)}), bf16[4,32,1024]{2,0,1:T(4,128)(2,1)}, u32[]{:S(2)}, u32[]{:S(2)}) async-start(bf16[4,32,1024]{2,0,1:T(4,128)(2,1)} %copy.540), calls=%async_computation.2 | async-start | bytes 524288 | tf_op jit(solution)/shard_map/all_to_all | solution.py:33
  52.6 3.1 %fusion.10 = f32[128,2048]{1,0:T(8,128)S(1)} fusion(bf16[128,1024]{1,0:T(8,128)(2,1)S(1)} %bitcast.122, bf16[1,1024,2048]{2,1,0:T(8,128)(2,1)} %param.7), kind=kOutput, calls=%fused_computation.10 | convolution fusion | flops 536870912 | bytes 5505024 | tf_op jit(solution)/shard_map/dot_general | solution.py:55
  55.9 1.6 fusion.21
  57.5 5.3 %all-to-all-done.2 = bf16[4,32,1024]{2,0,1:T(4,128)(2,1)} async-done(((bf16[4,32,1024]{2,0,1:T(4,128)(2,1)}), bf16[4,32,1024]{2,0,1:T(4,128)(2,1)}, u32[]{:S(2)}, u32[]{:S(2)}) %all-to-all-start.2) | async-done | bytes 262176 | tf_op jit(solution)/shard_map/all_to_all | solution.py:33
  62.8 1.0 copy.541
  63.9 4.9 %fusion.15 = bf16[128,2048]{1,0:T(8,128)(2,1)} fusion(bf16[128,1024]{1,0:T(8,128)(2,1)S(1)} %bitcast.124, bf16[1,2048,1024]{2,1,0:T(8,128)(2,1)} %param.8, f32[128,2048]{1,0:T(8,128)S(1)} %fusion.10), kind=kOutput, calls=%fused_computation.16 | convolution fusion | flops 541851648 | bytes 6029312 | tf_op jit(solution)/shard_map/rd,hd->rh/dot_general | solution.py:72
  68.8 0.9 copy.538
  69.7 3.3 %all-to-all-start.1 = ((bf16[4,32,1024]{2,0,1:T(4,128)(2,1)}), bf16[4,32,1024]{2,0,1:T(4,128)(2,1)}, u32[]{:S(2)}, u32[]{:S(2)}) async-start(bf16[4,32,1024]{2,0,1:T(4,128)(2,1)} %copy.538), calls=%async_computation.1 | async-start | bytes 524288 | tf_op jit(solution)/shard_map/all_to_all | solution.py:29
  73.1 3.9 %fusion.18 = bf16[128,1024]{1,0:T(8,128)(2,1)S(1)} fusion(bf16[128,2048]{1,0:T(8,128)(2,1)} %fusion.15, bf16[1,1024,2048]{2,1,0:T(8,128)(2,1)} %param.7), kind=kOutput, calls=%fused_computation.22 | convolution fusion | flops 537001984 | bytes 4980736 | tf_op jit(solution)/shard_map/rh,dh->rd/dot_general | solution.py:77
  77.0 0.9 copy.542
  77.9 3.3 %convert_bitcast_fusion.1 = bf16[1,1024,2048]{2,1,0:T(8,128)(2,1)} fusion(bf16[128,1024]{1,0:T(8,128)(2,1)S(1)} %bitcast.123, bf16[128,2048]{1,0:T(8,128)(2,1)S(1)} %copy-done.1), kind=kOutput, calls=%fused_computation.13 | convolution fusion | flops 538968064 | bytes 4980736 | tf_op jit(solution)/shard_map/rd,rh->dh/dot_general | solution.py:74
  81.2 3.3 %convert_bitcast_fusion = bf16[1,2048,1024]{2,1,0:T(8,128)(2,1)} fusion(bf16[128,1024]{1,0:T(8,128)(2,1)S(1)} %bitcast.125, f32[128,2048]{1,0:T(8,128)S(1)} %fusion.10), kind=kOutput, calls=%fused_computation.12 | convolution fusion | flops 541327360 | bytes 5505024 | tf_op jit(solution)/shard_map/rh,rd->hd/dot_general | solution.py:69
  84.5 5.8 %all-to-all-start.3 = ((bf16[4,32,1024]{2,0,1:T(4,128)(2,1)}), bf16[4,32,1024]{2,0,1:T(4,128)(2,1)S(1)}, u32[]{:S(2)}, u32[]{:S(2)}) async-start(bf16[4,32,1024]{2,0,1:T(4,128)(2,1)} %copy.542), calls=%async_computation.3 | async-start | bytes 524288 | tf_op jit(solution)/shard_map/all_to_all | solution.py:37
  90.5 2.4 %convolution_bitcast_fusion.1 = f32[4,256,32]{1,2,0:T(8,128)S(1)} fusion(bf16[4,256,1024]{2,1,0:T(8,128)(2,1)} %param.9, bf16[4,32,1024]{2,0,1:T(4,128)(2,1)} %all-to-all-done.1), kind=kOutput, calls=%fused_computation.27 | convolution fusion | flops 67108864 | bytes 2490368 | tf_op jit(solution)/shard_map/imd,isd->ims/dot_general | solution.py:67
  92.9 1.0 fusion.32
  94.0 6.7 %all-to-all-done.3 = bf16[4,32,1024]{2,0,1:T(4,128)(2,1)S(1)} async-done(((bf16[4,32,1024]{2,0,1:T(4,128)(2,1)}), bf16[4,32,1024]{2,0,1:T(4,128)(2,1)S(1)}, u32[]{:S(2)}, u32[]{:S(2)}) %all-to-all-start.3) | async-done | bytes 262176 | tf_op jit(solution)/shard_map/all_to_all | solution.py:37
  100.7 0.7 convolution_bitcast_fusion
  101.4 1.2 convolution_bitcast_fusion.2
  102.7 2.8 %fusion.46 = f32[4,256,1024]{2,1,0:T(8,128)} fusion(bf16[4,32,1024]{2,0,1:T(4,128)(2,1)S(1)} %all-to-all-done.3, f32[4,32]{1,0:T(4,128)S(1)} %get-tuple-element.37, f32[4,256,32]{1,2,0:T(8,128)S(1)} %fusion.52), kind=kOutput, calls=%fused_computation.49 | convolution fusion | flops 67207552 | bytes 4588032 | tf_op jit(solution)/shard_map/ims,isd->imd/dot_general | solution.py:86
  105.5 4.5 %add_convert_fusion = bf16[4,256,1024]{2,1,0:T(8,128)(2,1)} fusion(f32[4,256,1024]{2,1,0:T(8,128)} %fusion.46, f32[4,256,32]{1,2,0:T(8,128)S(1)} %fusion.32, f32[4,256,32]{1,2,0:T(8,128)S(1)} %convolution_bitcast_fusion, bf16[1024,32]{0,1:T(8,128)(2,1)S(1)} %copy-done.5, f32[4,256,32]{1,2,0:T(8,128)S(1)} %copy-done.4, f32[4,32]{1,0:T(4,128)S(1)} %get-tuple-element.37), kind=kOutput, calls=%fused_computation.14 | convolution fusion | flops 69435776 | bytes 6750720 | tf_op jit(solution)/shard_map/ims,ds->imd/dot_general | solution.py:87
  110.0 3.0 %convolution_convert_fusion = bf16[4,256,1024]{2,1,0:T(8,128)(2,1)} fusion(bf16[4,32,1024]{2,0,1:T(4,128)(2,1)} %all-to-all-done.1, f32[4,256]{1,0:T(4,128)S(1)} %get-tuple-element.39, f32[4,256,32]{1,2,0:T(8,128)S(1)} %fusion.52), kind=kOutput, calls=%fused_computation.17 | convolution fusion | flops 68256800 | bytes 2494464 | tf_op jit(solution)/shard_map/ims,isd->imd/dot_general | solution.py:60
  113.0 110.1 %all-reduce.3.cloned.1.call-done = f32[1024,32]{0,1:T(8,128)} async-done(((f32[1024,32]{0,1:T(8,128)}), f32[1024,32]{0,1:T(8,128)}) %all-reduce.3.cloned.1.call-update) | async-done | bytes 131088
  223.2 1.4 constant_dynamic-slice_fusion
  (37 shorter events, 10.8 us)
Async XLA Ops:
  7.2 1.6 copy-start
  31.5 17.7 %all-to-all-start = ((bf16[32,4,1,1024]{3,1,2,0:T(4,128)(2,1)}), bf16[32,4,1,1024]{3,1,2,0:T(4,128)(2,1)S(1)}, u32[]{:S(2)}, u32[]{:S(2)}) async-start(bf16[32,4,1,1024]{3,1,2,0:T(4,128)(2,1)} %constant_dynamic-update-slice_fusion), calls=%async_computation | async-start | bytes 524288 | tf_op jit(solution)/shard_map/all_to_all | solution.py:21
  49.2 13.7 %all-to-all-start.2 = ((bf16[4,32,1024]{2,0,1:T(4,128)(2,1)}), bf16[4,32,1024]{2,0,1:T(4,128)(2,1)}, u32[]{:S(2)}, u32[]{:S(2)}) async-start(bf16[4,32,1024]{2,0,1:T(4,128)(2,1)} %copy.540), calls=%async_computation.2 | async-start | bytes 524288 | tf_op jit(solution)/shard_map/all_to_all | solution.py:33
  52.5 3.5 %copy-start.7 = (bf16[1,2048,1024]{2,1,0:T(8,128)(2,1)S(1)}, bf16[1,2048,1024]{2,1,0:T(8,128)(2,1)}, u32[]{:S(2)}) copy-start(bf16[1,2048,1024]{2,1,0:T(8,128)(2,1)} %param.8) | copy-start | bytes 12582916
  63.9 4.9 %copy-start.2 = (bf16[4,32,1024]{2,1,0:T(8,128)(2,1)}, bf16[4,32,1024]{2,1,0:T(8,128)(2,1)S(1)}, u32[]{:S(2)}) copy-start(bf16[4,32,1024]{2,1,0:T(8,128)(2,1)S(1)} %copy.541) | copy-start | bytes 786436
  63.9 4.9 %copy-start.6 = (bf16[128,1024]{1,0:T(8,128)(2,1)S(1)}, bf16[128,1024]{1,0:T(8,128)(2,1)}, u32[]{:S(2)}) copy-start(bf16[128,1024]{1,0:T(8,128)(2,1)} %fusion.21) | copy-start | bytes 786436
  69.7 14.8 %all-to-all-start.1 = ((bf16[4,32,1024]{2,0,1:T(4,128)(2,1)}), bf16[4,32,1024]{2,0,1:T(4,128)(2,1)}, u32[]{:S(2)}, u32[]{:S(2)}) async-start(bf16[4,32,1024]{2,0,1:T(4,128)(2,1)} %copy.538), calls=%async_computation.1 | async-start | bytes 524288 | tf_op jit(solution)/shard_map/all_to_all | solution.py:29
  73.0 4.9 %copy-start.1 = (bf16[128,2048]{1,0:T(8,128)(2,1)S(1)}, bf16[128,2048]{1,0:T(8,128)(2,1)}, u32[]{:S(2)}) copy-start(bf16[128,2048]{1,0:T(8,128)(2,1)} %fusion.15) | copy-start | bytes 1572868
  73.0 8.1 %copy-start.3 = (bf16[4,32,1024]{2,1,0:T(8,128)(2,1)S(1)}, bf16[4,32,1024]{2,1,0:T(8,128)(2,1)}, u32[]{:S(2)}) copy-start(bf16[4,32,1024]{2,1,0:T(8,128)(2,1)} %copy-done.2) | copy-start | bytes 786436
  84.5 16.9 %copy-start.4 = (f32[4,256,32]{1,2,0:T(8,128)S(1)}, f32[4,256,32]{1,2,0:T(8,128)}, u32[]{:S(2)}) copy-start(f32[4,256,32]{1,2,0:T(8,128)} %get-tuple-element.38) | copy-start | bytes 393220
  84.5 16.2 %all-to-all-start.3 = ((bf16[4,32,1024]{2,0,1:T(4,128)(2,1)}), bf16[4,32,1024]{2,0,1:T(4,128)(2,1)S(1)}, u32[]{:S(2)}, u32[]{:S(2)}) async-start(bf16[4,32,1024]{2,0,1:T(4,128)(2,1)} %copy.542), calls=%async_computation.3 | async-start | bytes 524288 | tf_op jit(solution)/shard_map/all_to_all | solution.py:37
  90.3 132.9 %all-reduce.3.cloned.1.call-start = ((), (), s32[]{:S(2)}) async-start(), calls=%async_computation.4 | async-start | bytes 262144
  94.0 11.6 %copy-start.5 = (bf16[1024,32]{0,1:T(8,128)(2,1)S(1)}, bf16[1024,32]{0,1:T(8,128)(2,1)}, u32[]{:S(2)}) copy-start(bf16[1024,32]{0,1:T(8,128)(2,1)} %param.6) | copy-start | bytes 196612
Sparse Core Ops, SparseCore 0:
  102.8 120.3 all-reduce.2
